TPU v7x, 32 devices: a whole 2x2x4 slice. The times are simulated.
32 devices in a mesh: parts: 2 (over x), wide: 16 (over z, y, core).
Axes of the slice: x: 2, y: 2, z: 4, core: 2. Of those that a mesh axis runs over, the one named last changes fastest.
Arguments:
- embeddings: bfloat16 [16384, 1024], P(('parts', 'wide')), parts along dimension 0, may hold values from -6 to 6
- cluster_id: int32 [16384, 1], P(('parts', 'wide')), parts along dimension 0, may hold values from 0 to 31; in each aligned block of 512 rows (0 to 511, 512 to 1023, ...) at most 32 rows name the same one
Outputs:
- similarity: float32 [16384], P(('parts', 'wide')), parts along dimension 0
There are 2 independent parts, one for each index of `parts`. A program takes and returns all parts, laid end to end along the dimension named above; each array names one. Nothing has to cross between parts.
Inputs may be any that keep to these rules, and one draw needn't show every extreme that they name: The cluster of row r is cluster_id[r, 0]; cluster c belongs to device c // 2 of the wide axis. In each aligned block of 512 rows (the rows of one device) no cluster is named by more than 32 rows.
All inputs are finite; a program needn't handle non-finite values.
Results may differ from a plain program's by a relative error of at most 0.0013.
Values may be sent and summed in bfloat16 or wider, within the bound.
A program may use at most 64 MiB of HBM per device.

v0:
```python
import jax
import jax.numpy as jnp
from jax import lax
from jax.sharding import PartitionSpec as P

CLUS_DEV = 2


def normalize(values):
    widened = values.astype(jnp.float32)
    scale = lax.rsqrt(jnp.sum(widened * widened, axis=-1, keepdims=True) + 1e-06)
    return (widened * scale).astype(jnp.bfloat16)


def per_device(embeddings, cluster_id):
    row_count = embeddings.shape[0]
    wide_count = lax.axis_size("wide")
    per_owner = CLUS_DEV
    capacity = 2 * row_count // (per_owner * wide_count)
    cluster_count = per_owner * wide_count
    total_slots = cluster_count * capacity
    cluster_ids = cluster_id[:, 0]
    onehot = (cluster_ids[:, None] == jnp.arange(cluster_count, dtype=jnp.int32)[None, :]).astype(
        jnp.int32
    )
    earlier = jnp.cumsum(onehot, axis=0) - onehot
    place_rank = jnp.sum(earlier * onehot, axis=1)
    slot_index = cluster_ids * capacity + place_rank
    source_row = (
        jnp.zeros((total_slots,), jnp.int32)
        .at[slot_index]
        .set(jnp.arange(row_count, dtype=jnp.int32))
    )
    filled_flags = jnp.zeros((total_slots,), jnp.bfloat16).at[slot_index].set(jnp.bfloat16(1.0))
    packed = embeddings[source_row].reshape(wide_count, per_owner, capacity, embeddings.shape[1])
    flag_blocks = filled_flags.reshape(wide_count, per_owner, capacity)
    received = lax.all_to_all(packed, "wide", split_axis=0, concat_axis=2, tiled=True)
    flags_here = lax.all_to_all(flag_blocks, "wide", split_axis=0, concat_axis=2, tiled=True)
    unit = normalize(received)
    slot_total = unit.shape[2]
    live = flags_here > 0
    gram = jnp.einsum("pksd,pktd->pkst", unit, unit, preferred_element_type=jnp.float32)
    positions = jnp.arange(slot_total, dtype=jnp.int32)
    mask = (positions[None, :] < positions[:, None])[None, None] & live[:, :, None, :]
    maxima = jnp.max(jnp.where(mask, gram, jnp.float32(-1.0)), axis=3)
    returned = lax.all_to_all(maxima, "wide", split_axis=2, concat_axis=0, tiled=True)
    return returned.reshape(total_slots)[slot_index]


def solution(mesh):
    in_specs = (P(("parts", "wide"), None), P(("parts", "wide"), None))
    out_specs = P(("parts", "wide"))
    return jax.shard_map(
        per_device, mesh=mesh, in_specs=in_specs, out_specs=out_specs, check_vma=False
    )
```

profile of v0, /device:TPU:0, one launch (start us, length us, event | category | flops | bytes accessed | tf_op | source)
XLA Modules:
  0.0 99.1 jit_solution(1852046851542584849)
XLA Ops:
  0.0 0.8 fusion.4
  0.8 1.2 %reduce-window.6 = s32[32,4,128]{2,0,1:T(8,128)S(1)} reduce-window(s32[32,4,128]{2,0,1:T(8,128)S(1)} %fusion.4, s32[]{:T(128)} %constant.12.clone.1), window={size=1x1x128 pad=0_0x0_0x127_0}, to_apply=%region_0.0 | reduce-window | flops 2080768 | bytes 131076 | tf_op jit(solution)/shard_map/reduce-window
  1.9 0.2 slice_reduce_fusion
  2.2 0.8 fusion.3
  3.0 0.7 compare_select_fusion
  3.7 3.8 %scatter_custom_fusion = bf16[1024]{0:T(1024)(128)(2,1)S(1)} fusion(s32[512]{0:T(512)S(1)} %bitcast.54, bf16[512]{0:T(512)(128)(2,1)S(1)} %broadcast.67, bf16[]{:T(256)} %constant.10.clone.1), kind=kCustom, calls=%fused_computation.28 | custom fusion | bytes 2050 | tf_op jit(solution)/shard_map/scatter | solution.py:34
  7.5 0.7 reshape.95
  8.1 7.4 %all-to-all-start = ((bf16[16,2,32]{2,1,0:T(2,128)(2,1)}), bf16[16,2,32]{2,1,0:T(2,128)(2,1)S(1)}, u32[]{:S(2)}, u32[]{:S(2)}) async-start(bf16[16,2,32]{2,1,0:T(2,128)(2,1)} %reshape.95), calls=%async_computation | async-start | bytes 16384 | tf_op jit(solution)/shard_map/all_to_all | solution.py:38
  15.5 2.4 %scatter_custom_fusion.1 = s32[1024]{0:T(1024)S(1)} fusion(s32[512]{0:T(512)S(1)} %bitcast.55, s32[512]{0:T(512)S(1)} %iota.25, s32[]{:T(128)} %constant.12.clone.1), kind=kCustom, calls=%fused_computation.26 | custom fusion | bytes 4100 | tf_op jit(solution)/shard_map/scatter | solution.py:32
  18.0 5.4 %gather_fusion = bf16[1024,1024]{1,0:T(8,128)(2,1)} fusion(bf16[512,1024]{1,0:T(8,128)(2,1)S(1)} %copy-done, s32[1024]{0:T(1024)S(1)} %fusion.5), kind=kCustom, calls=%fused_computation | custom fusion | bytes 4198400 | tf_op jit(solution)/shard_map/gather | solution.py:35
  23.4 6.0 %all-to-all-start.1 = ((bf16[16,2,32,1024]{3,2,1,0:T(8,128)(2,1)}), bf16[16,2,32,1024]{3,2,1,0:T(8,128)(2,1)S(1)}, u32[]{:S(2)}, u32[]{:S(2)}) async-start(bf16[16,2,32,1024]{3,2,1,0:T(8,128)(2,1)} %bitcast.48), calls=%async_computation.1 | async-start | bytes 4194304 | tf_op jit(solution)/shard_map/all_to_all | solution.py:37
  29.5 0.1 gt.25
  29.6 40.9 %all-to-all-done.1 = bf16[16,2,32,1024]{3,2,1,0:T(8,128)(2,1)S(1)} async-done(((bf16[16,2,32,1024]{3,2,1,0:T(8,128)(2,1)}), bf16[16,2,32,1024]{3,2,1,0:T(8,128)(2,1)S(1)}, u32[]{:S(2)}, u32[]{:S(2)}) %all-to-all-start.1) | async-done | bytes 2097184 | tf_op jit(solution)/shard_map/all_to_all | solution.py:37
  70.5 0.5 multiply_reduce_fusion
  71.0 0.1 rsqrt.12
  71.1 0.5 copy_convert_fusion
  71.6 0.3 fusion
  71.9 1.4 %select_reduce_fusion = f32[2,512]{1,0:T(2,128)S(1)} fusion(bf16[2,512,1024]{2,1,0:T(8,128)(2,1)S(1)} %fusion, pred[2,512]{1,0:T(4,128)(4,1)S(1)} %gt.25, pred[512,512]{0,1:T(8,128)(4,1)S(1)} %iota_compare_fusion), kind=kOutput, calls=%fused_computation.8 | convolution fusion | flops 1075313664 | bytes 2364416 | tf_op jit(solution)/shard_map/pksd,pktd->pkst/dot_general | solution.py:42
  73.3 0.9 copy.26
  74.1 11.2 %all-to-all-start.2 = ((f32[1,2,512]{1,0,2:T(1,128)}), f32[1,2,512]{1,0,2:T(1,128)S(1)}, u32[]{:S(2)}, u32[]{:S(2)}) async-start(f32[1,2,512]{1,0,2:T(1,128)} %copy.26), calls=%async_computation.2 | async-start | bytes 524288 | tf_op jit(solution)/shard_map/all_to_all | solution.py:46
  85.3 10.0 %all-to-all-done.2 = f32[1,2,512]{1,0,2:T(1,128)S(1)} async-done(((f32[1,2,512]{1,0,2:T(1,128)}), f32[1,2,512]{1,0,2:T(1,128)S(1)}, u32[]{:S(2)}, u32[]{:S(2)}) %all-to-all-start.2) | async-done | bytes 4128 | tf_op jit(solution)/shard_map/all_to_all | solution.py:46
  95.4 0.2 copy.29
  95.6 0.1 reshape.97
  95.6 3.4 %gather_fusion.1 = f32[512]{0:T(512)} fusion(f32[1024]{0:T(1024)S(1)} %reshape.97, s32[1024]{0:T(1024)S(1)} %pad_clamp_fusion), kind=kCustom, calls=%fused_computation.1 | custom fusion | bytes 6144 | tf_op jit(solution)/shard_map/gather | solution.py:47
  (16 shorter events, 0.2 us)
Async XLA Ops:
  0.0 18.0 %copy-start = (bf16[512,1024]{1,0:T(8,128)(2,1)S(1)}, bf16[512,1024]{1,0:T(8,128)(2,1)}, u32[]{:S(2)}) copy-start(bf16[512,1024]{1,0:T(8,128)(2,1)} %param.2) | copy-start | bytes 3145732
  8.1 15.2 %all-to-all-start = ((bf16[16,2,32]{2,1,0:T(2,128)(2,1)}), bf16[16,2,32]{2,1,0:T(2,128)(2,1)S(1)}, u32[]{:S(2)}, u32[]{:S(2)}) async-start(bf16[16,2,32]{2,1,0:T(2,128)(2,1)} %reshape.95), calls=%async_computation | async-start | bytes 16384 | tf_op jit(solution)/shard_map/all_to_all | solution.py:38
  23.4 47.1 %all-to-all-start.1 = ((bf16[16,2,32,1024]{3,2,1,0:T(8,128)(2,1)}), bf16[16,2,32,1024]{3,2,1,0:T(8,128)(2,1)S(1)}, u32[]{:S(2)}, u32[]{:S(2)}) async-start(bf16[16,2,32,1024]{3,2,1,0:T(8,128)(2,1)} %bitcast.48), calls=%async_computation.1 | async-start | bytes 4194304 | tf_op jit(solution)/shard_map/all_to_all | solution.py:37
  74.1 21.3 %all-to-all-start.2 = ((f32[1,2,512]{1,0,2:T(1,128)}), f32[1,2,512]{1,0,2:T(1,128)S(1)}, u32[]{:S(2)}, u32[]{:S(2)}) async-start(f32[1,2,512]{1,0,2:T(1,128)} %copy.26), calls=%async_computation.2 | async-start | bytes 524288 | tf_op jit(solution)/shard_map/all_to_all | solution.py:46
where the time goes:
time: 99.5 us; the launch traced here: 99.1 us
  waiting for transfers between devices  50.9 us (51%)
  starting transfers between devices  24.6 us (25%)
  local copies, waits for them, and re-layouts  17.2 us (17%)
  other arithmetic  4.81 us (5%)
  matrix products  1.36 us (1%)
    all_to_all x1, waiting for transfers between devices, per_device(): lax.all_to_all(packed, 'wide', split_axis=0, concat_axis=2, tiled=True)  40.9 us
    all_to_all x1, starting transfers between devices, per_device(): lax.all_to_all(maxima, 'wide', split_axis=2, concat_axis=0, tiled=True)  11.2 us
    all_to_all x1, waiting for transfers between devices, per_device(): lax.all_to_all(maxima, 'wide', split_axis=2, concat_axis=0, tiled=True)  10 us
    all_to_all x1, starting transfers between devices, per_device(): lax.all_to_all(flag_blocks, 'wide', split_axis=0, concat_axis=2, tiled=True)  7.39 us
    all_to_all x1, starting transfers between devices, per_device(): lax.all_to_all(packed, 'wide', split_axis=0, concat_axis=2, tiled=True)  6.01 us
    gather x1, local copies, waits for them, and re-layouts, per_device(): embeddings[source_row]  5.36 us
    scatter x1, local copies, waits for them, and re-layouts, per_device(): jnp.zeros((total_slots,), jnp.bfloat16).at[slot_index]  3.77 us
    gather x1, local copies, waits for them, and re-layouts, per_device(): return returned.reshape(total_slots)[slot_index]  3.41 us
  transfers between devices with their start and end apart: 3, of which 2 were waited for; matrix products, arithmetic and copies ran while one was open for 8% of the time, Pallas kernels for 0%

commit v1 on v0

--- a/solution.py
+++ b/solution.py
@@ -1,9 +1,16 @@
+import functools
+
 import jax
 import jax.numpy as jnp
 from jax import lax
+from jax.experimental import pallas as pl
+from jax.experimental.pallas import tpu as pltpu
 from jax.sharding import PartitionSpec as P
 
 CLUS_DEV = 2
+LANES = 128
+EMPTY = 4.0
+FAR = 1 << 20
 
 
 def normalize(values):
@@ -12,7 +19,206 @@
     return (widened * scale).astype(jnp.bfloat16)
 
 
-def per_device(embeddings, cluster_id):
+def dispatch_kernel(
+    n, cap, emb_ref, cid_ref, out_ref, unit, send, recv, res, ret,
+    send_sem, recv_sem, back_send_sem, back_recv_sem,
+):
+    me = lax.axis_index("wide")
+    rows, width = emb_ref.shape
+    block = CLUS_DEV * cap
+    slots = n * cap
+    clusters = CLUS_DEV * n
+
+    def peer(k):
+        return lax.rem(me + k, n)
+
+    barrier = pltpu.get_barrier_semaphore()
+
+    def greet(k, carry):
+        pl.semaphore_signal(
+            barrier, inc=1, device_id={"wide": peer(k)}, device_id_type=pl.DeviceIdType.MESH
+        )
+        return carry
+
+    lax.fori_loop(1, n, greet, 0)
+
+    def unit_rows(t, carry):
+        part = pl.ds(pl.multiple_of(t * 64, 64), 64)
+        unit[part, :] = normalize(emb_ref[part, :])
+        return carry
+
+    lax.fori_loop(0, rows // 64, unit_rows, 0)
+    cid = cid_ref[...]
+    named = lax.broadcasted_iota(jnp.int32, (clusters, rows), 0) == cid
+    before = lax.broadcasted_iota(jnp.int32, (rows, rows), 0) < lax.broadcasted_iota(
+        jnp.int32, (rows, rows), 1
+    )
+    earlier = jnp.dot(
+        jnp.where(named, 1.0, 0.0).astype(jnp.bfloat16),
+        jnp.where(before, 1.0, 0.0).astype(jnp.bfloat16),
+        preferred_element_type=jnp.float32,
+    )
+    rank = jnp.sum(jnp.where(named, earlier, 0.0), axis=0, keepdims=True).astype(jnp.int32)
+    slot = cid * cap + rank
+
+    pl.semaphore_wait(barrier, n - 1)
+
+    def block_copy(k, place):
+        return pltpu.make_async_remote_copy(
+            src_ref=send.at[place],
+            dst_ref=recv.at[me],
+            send_sem=send_sem.at[k],
+            recv_sem=recv_sem.at[k],
+            device_id={"wide": peer(k)},
+            device_id_type=pl.DeviceIdType.MESH,
+        )
+
+    order = sorted(range(n), key=lambda k: (abs(k - n // 2), k))
+    group = 4
+    for first in range(0, n, group):
+        chosen = order[first:first + group]
+        picks = jnp.concatenate(
+            [
+                jnp.where(
+                    lax.broadcasted_iota(jnp.int32, (block, rows), 0) + peer(k) * block == slot,
+                    1.0,
+                    0.0,
+                )
+                for k in chosen
+            ],
+            axis=0,
+        )
+        packed = jnp.dot(
+            picks.astype(jnp.bfloat16), unit[...], preferred_element_type=jnp.float32
+        ).astype(jnp.bfloat16)
+        filled = jnp.max(picks, axis=1, keepdims=True)
+        head = packed[:, :LANES].astype(jnp.float32)
+        marked = (lax.broadcasted_iota(jnp.int32, head.shape, 1) == 0) & (filled < 0.5)
+        head = jnp.where(marked, EMPTY, head).astype(jnp.bfloat16)
+        for i, k in enumerate(chosen):
+            part = slice(i * block, (i + 1) * block)
+            if k == 0:
+                recv[me, :, :LANES] = head[part]
+                recv[me, :, LANES:] = packed[part, LANES:]
+            else:
+                send[first + i, :, :LANES] = head[part]
+                send[first + i, :, LANES:] = packed[part, LANES:]
+                block_copy(k, first + i).start()
+
+    def arrived(k, carry):
+        pltpu.make_async_remote_copy(
+            src_ref=send.at[0],
+            dst_ref=recv.at[lax.rem(me + n - k, n)],
+            send_sem=send_sem.at[k],
+            recv_sem=recv_sem.at[k],
+            device_id={"wide": peer(k)},
+            device_id_type=pl.DeviceIdType.MESH,
+        ).wait_recv()
+        return carry
+
+    lax.fori_loop(1, n, arrived, 0)
+
+    step = 256
+    for c in range(CLUS_DEV):
+        for start in range(0, slots, step):
+            top = start + step
+            keys = recv[: top // cap, c * cap:(c + 1) * cap, :].reshape(top, width)
+            queries = recv[start // cap:top // cap, c * cap:(c + 1) * cap, :].reshape(step, width)
+            gram = lax.dot_general(
+                keys, queries, (((1,), (1,)), ((), ())), preferred_element_type=jnp.float32
+            )
+            flag = keys[:, :LANES].astype(jnp.float32)[:, :1]
+            position = lax.broadcasted_iota(jnp.int32, (top, 1), 0)
+            position = jnp.where(flag < 2.0, position, FAR)
+            mine = lax.broadcasted_iota(jnp.int32, (1, step), 1) + start
+            best = jnp.max(jnp.where(position < mine, gram, -1.0), axis=0, keepdims=True)
+            for lane in range(0, step, LANES):
+                row = (c * slots + start + lane) // LANES
+                res[row:row + 1, :] = best[:, lane:lane + LANES]
+
+    def back_copy(k):
+        return pltpu.make_async_remote_copy(
+            src_ref=res,
+            dst_ref=ret.at[me],
+            send_sem=back_send_sem.at[k],
+            recv_sem=back_recv_sem.at[k],
+            device_id={"wide": peer(k)},
+            device_id_type=pl.DeviceIdType.MESH,
+        )
+
+    def give_back(k, carry):
+        back_copy(k).start()
+        return carry
+
+    lax.fori_loop(1, n, give_back, 0)
+    ret[me] = res[...]
+
+    def sent(k, carry):
+        block_copy(k, 0).wait_send()
+        return carry
+
+    lax.fori_loop(1, n, sent, 0)
+
+    def returned(k, carry):
+        pltpu.make_async_remote_copy(
+            src_ref=res,
+            dst_ref=ret.at[lax.rem(me + n - k, n)],
+            send_sem=back_send_sem.at[k],
+            recv_sem=back_recv_sem.at[k],
+            device_id={"wide": peer(k)},
+            device_id_type=pl.DeviceIdType.MESH,
+        ).wait()
+        return carry
+
+    lax.fori_loop(1, n, returned, 0)
+
+    lines = clusters * slots // LANES
+    value = ret[...].reshape(lines, LANES)
+    place = me * cap
+    line = cid * (slots // LANES) + lax.div(place, LANES)
+    lane = rank + lax.rem(place, LANES)
+    chosen = (lax.broadcasted_iota(jnp.int32, (lines, rows), 0) == line)
+    chosen = jnp.where(chosen, 1.0, 0.0).astype(jnp.bfloat16)
+    looked = jnp.zeros((LANES, rows), jnp.float32)
+    for _ in range(3):
+        piece = value.astype(jnp.bfloat16)
+        looked = looked + lax.dot_general(
+            piece, chosen, (((0,), (0,)), ((), ())), preferred_element_type=jnp.float32
+        )
+        value = value - piece.astype(jnp.float32)
+    at_lane = lax.broadcasted_iota(jnp.int32, (LANES, rows), 0) == lane
+    out_ref[...] = jnp.sum(jnp.where(at_lane, looked, 0.0), axis=0, keepdims=True)
+
+
+def by_kernel(embeddings, cluster_id):
+    rows, width = embeddings.shape
+    n = lax.axis_size("wide")
+    cap = 2 * rows // (CLUS_DEV * n)
+    lines = CLUS_DEV * n * cap // LANES
+    out = pl.pallas_call(
+        functools.partial(dispatch_kernel, n, cap),
+        out_shape=jax.ShapeDtypeStruct((1, rows), jnp.float32),
+        in_specs=[pl.BlockSpec(memory_space=pltpu.VMEM)] * 2,
+        out_specs=pl.BlockSpec(memory_space=pltpu.VMEM),
+        scratch_shapes=[
+            pltpu.VMEM((rows, width), jnp.bfloat16),
+            pltpu.VMEM((n, CLUS_DEV * cap, width), jnp.bfloat16),
+            pltpu.VMEM((n, CLUS_DEV * cap, width), jnp.bfloat16),
+            pltpu.VMEM((lines, LANES), jnp.float32),
+            pltpu.VMEM((n, lines, LANES), jnp.float32),
+            pltpu.SemaphoreType.DMA((n,)),
+            pltpu.SemaphoreType.DMA((n,)),
+            pltpu.SemaphoreType.DMA((n,)),
+            pltpu.SemaphoreType.DMA((n,)),
+        ],
+        compiler_params=pltpu.CompilerParams(
+            collective_id=0, has_side_effects=True, vmem_limit_bytes=40 << 20
+        ),
+    )(embeddings, cluster_id.reshape(1, rows))
+    return out.reshape(rows)
+
+
+def by_collectives(embeddings, cluster_id):
     row_count = embeddings.shape[0]
     wide_count = lax.axis_size("wide")
     per_owner = CLUS_DEV
@@ -47,6 +253,15 @@
     return returned.reshape(total_slots)[slot_index]
 
 
+def per_device(embeddings, cluster_id):
+    rows, width = embeddings.shape
+    n = lax.axis_size("wide")
+    cap = 2 * rows // (CLUS_DEV * n)
+    if cap % 16 == 0 and n % 4 == 0 and (n * cap) % 256 == 0 and 256 % cap == 0 and width % LANES == 0:
+        return by_kernel(embeddings, cluster_id)
+    return by_collectives(embeddings, cluster_id)
+
+
 def solution(mesh):
     in_specs = (P(("parts", "wide"), None), P(("parts", "wide"), None))
     out_specs = P(("parts", "wide"))

time: 99.5 us -> 61.9 us (0.62)
  Pallas kernels: 0 us -> 59.3 us
  waiting for transfers between devices: 50.9 us -> 0 us
  starting transfers between devices: 24.6 us -> 0 us
  local copies, waits for them, and re-layouts: 17.2 us -> 2.49 us
  other arithmetic: 4.81 us -> 0 us
  matrix products: 1.36 us -> 0 us
    pallas_call x0 -> x1, Pallas kernels: none -> 59.3 us  [by_kernel(): pl.pallas_call(functools.partial(dispatch_kernel, n, cap), out_shape=jax....]
    all_to_all x3 -> x0, waiting for transfers between devices: 50.9 us -> none  [the longest x1 40.9 us: per_device(): lax.all_to_all(packed, 'wide', split_axis=0, concat_axis=2, tiled=True)]
    all_to_all x3 -> x0, starting transfers between devices: 24.6 us -> none  [the longest x1 11.2 us: per_device(): lax.all_to_all(maxima, 'wide', split_axis=2, concat_axis=0, tiled=True)]
    gather x2 -> x0, local copies, waits for them, and re-layouts: 8.77 us -> none  [the longest x1 5.36 us: per_device(): embeddings[source_row]]
    scatter x2 -> x0, local copies, waits for them, and re-layouts: 6.21 us -> none  [the longest x1 3.77 us: per_device(): jnp.zeros((total_slots,), jnp.bfloat16).at[slot_index]]
    unnamed x3 -> x5, local copies, waits for them, and re-layouts: 0.01 us -> 2.49 us
    convert_element_type x3 -> x0, other arithmetic: 1.55 us -> none  [the longest x1 0.78 us: per_device(): (cluster_ids[:, None] == jnp.arange(cluster_count, dtype=jnp.int32)[None,...]
    dot_general x1 -> x0, matrix products: 1.36 us -> none  [per_device(): jnp.einsum('pksd,pktd->pkst', unit, unit, preferred_element_type=jnp.floa...]
  transfers between devices with their start and end apart: 3 -> 0, of which waited for: 2 -> 0; matrix products, arithmetic and copies ran while one was open for 8% -> 0% of each run, Pallas kernels for 0% -> 0%
where the time goes in v1:
time: 61.9 us; the launch traced here: 61.7 us
  Pallas kernels  59.3 us (96%)
  local copies, waits for them, and re-layouts  2.49 us (4%)
    pallas_call x1, Pallas kernels, by_kernel(): pl.pallas_call(functools.partial(dispatch_kernel, n, cap), out_shape=jax....  59.3 us
    unnamed x5, local copies, waits for them, and re-layouts  2.49 us

profile of v1, /device:TPU:0, one launch (start us, length us, event | category | flops | bytes accessed | tf_op | source)
XLA Modules:
  0.0 61.7 jit_solution(1858552759152495997)
XLA Ops:
  0.0 0.0 copy-start
  0.0 1.2 %copy-done = bf16[512,1024]{1,0:T(8,128)(2,1)S(1)} copy-done((bf16[512,1024]{1,0:T(8,128)(2,1)S(1)}, bf16[512,1024]{1,0:T(8,128)(2,1)}, u32[]{:S(2)}) %copy-start) | copy-done | bytes 1048600
  1.2 0.0 copy-start.1
  1.2 0.7 %copy-done.1 = s32[512,1]{0,1:T(1,128)S(1)} copy-done((s32[512,1]{0,1:T(1,128)S(1)}, s32[512,1]{0,1:T(1,128)}, u32[]{:S(2)}) %copy-start.1) | copy-done | bytes 2072
  1.9 59.3 %shard_map.28 = f32[1,512]{1,0:T(1,128)S(1)} custom-call(bf16[512,1024]{1,0:T(8,128)(2,1)S(1)} %copy-done, s32[1,512]{1,0:T(1,128)S(1)} %bitcast.3), custom_call_target="tpu_custom_call" | custom-call | tf_op jit(solution)/shard_map/pallas_call | solution.py:198
  61.2 0.6 copy.4
Async XLA Ops:
  0.0 1.2 %copy-start = (bf16[512,1024]{1,0:T(8,128)(2,1)S(1)}, bf16[512,1024]{1,0:T(8,128)(2,1)}, u32[]{:S(2)}) copy-start(bf16[512,1024]{1,0:T(8,128)(2,1)} %emb_ref.1) | copy-start | bytes 3145732
  1.2 0.7 %copy-start.1 = (s32[512,1]{0,1:T(1,128)S(1)}, s32[512,1]{0,1:T(1,128)}, u32[]{:S(2)}) copy-start(s32[512,1]{0,1:T(1,128)} %param.3) | copy-start | bytes 6148

commit v2 on v1

v2 whole, which is shorter than its diff:
```python
import functools

import jax
import jax.numpy as jnp
from jax import lax
from jax.experimental import pallas as pl
from jax.experimental.pallas import tpu as pltpu
from jax.sharding import PartitionSpec as P

CLUS_DEV = 2
LANES = 128
EMPTY = 1024.0
CHUNKS = 4
FAR = 1 << 20


def normalize(values):
    widened = values.astype(jnp.float32)
    scale = lax.rsqrt(jnp.sum(widened * widened, axis=-1, keepdims=True) + 1e-06)
    return (widened * scale).astype(jnp.bfloat16)


def ranks(cid, clusters):
    rows = cid.shape[1]
    named = lax.broadcasted_iota(jnp.int32, (clusters, rows), 0) == cid
    before = lax.broadcasted_iota(jnp.int32, (rows, rows), 0) < lax.broadcasted_iota(
        jnp.int32, (rows, rows), 1
    )
    earlier = jnp.dot(
        jnp.where(named, 1.0, 0.0).astype(jnp.bfloat16),
        jnp.where(before, 1.0, 0.0).astype(jnp.bfloat16),
        preferred_element_type=jnp.float32,
    )
    return jnp.sum(jnp.where(named, earlier, 0.0), axis=0, keepdims=True).astype(jnp.int32)


def dispatch_kernel(
    n, cap, emb_ref, cid_ref, out_ref, stage, ids, send, recv, res, ret, picked,
    local_sem, move_send_sem, move_recv_sem, id_sem, send_sem, recv_sem, back_send_sem,
    back_recv_sem,
):
    part = lax.axis_index("parts")
    wide = lax.axis_index("wide")
    half = n // 2
    side = lax.div(wide, half)
    spot = lax.rem(wide, half)
    core = lax.rem(wide, 2)
    away = lax.rem(part + side + 1, 2)
    home = 1 - away
    me = part * half + spot
    guest = 1 - side
    keeps = (home == 1) & (core == 0)
    crosses = lax.rem(home + core, 2) == 1
    rows, width = emb_ref.shape
    block = CLUS_DEV * cap
    slots = n * cap
    clusters = CLUS_DEV * n

    def device(part_of, wide_of):
        return {"parts": part_of, "wide": wide_of}

    def in_cube(index):
        return device(lax.div(index, half), side * half + lax.rem(index, half))

    def block_of(index):
        x, t = lax.div(index, half), lax.rem(index, half)
        flip = lax.rem(x + side + 1 + lax.rem(t, 2), 2)
        return lax.rem(side + flip, 2) * half + t

    def peer(k):
        return lax.rem(me + k, n)

    barrier = pltpu.get_barrier_semaphore()
    everyone = 2 * n

    def greet(k, carry):
        other = lax.rem(part * n + wide + k, everyone)
        pl.semaphore_signal(
            barrier,
            inc=1,
            device_id=device(lax.div(other, n), lax.rem(other, n)),
            device_id_type=pl.DeviceIdType.MESH,
        )
        return carry

    lax.fori_loop(1, everyone, greet, 0)
    own_ids = pltpu.make_async_copy(cid_ref, ids.at[0], local_sem.at[0])
    own_rows = pltpu.make_async_copy(emb_ref, stage.at[0], local_sem.at[1])
    own_ids.start()
    own_rows.start()
    own_ids.wait()
    own_rows.wait()
    own_cid = ids[0]
    own_rank = ranks(own_cid, clusters)

    chunk = rows // CHUNKS
    next_part = jnp.where(crosses, part, 1 - part)
    next_wide = jnp.where(crosses, (1 - side) * half + spot, wide)

    def move(q, source):
        piece = pl.ds(q * chunk, chunk)
        return pltpu.make_async_remote_copy(
            src_ref=stage.at[source, piece],
            dst_ref=stage.at[1, piece],
            send_sem=move_send_sem.at[q],
            recv_sem=move_recv_sem.at[q],
            device_id=device(next_part, next_wide),
            device_id_type=pl.DeviceIdType.MESH,
        )

    def move_ids(source):
        return pltpu.make_async_remote_copy(
            src_ref=ids.at[source],
            dst_ref=ids.at[1],
            send_sem=id_sem.at[0],
            recv_sem=id_sem.at[1],
            device_id=device(next_part, next_wide),
            device_id_type=pl.DeviceIdType.MESH,
        )

    pl.semaphore_wait(barrier, everyone - 1)

    @pl.when(jnp.logical_not(keeps))
    def _():
        move_ids(0).start()
        for q in range(CHUNKS):
            move(q, 0).start()
        move_ids(0).wait_recv()
        for q in range(CHUNKS):
            move(q, 0).wait_recv()

    held = jnp.where(keeps, 0, 1)
    cid = ids[held]
    slot = cid * cap + ranks(cid, clusters)
    place = block_of(me)

    def block_copy(k):
        return pltpu.make_async_remote_copy(
            src_ref=send.at[k],
            dst_ref=recv.at[place],
            send_sem=send_sem.at[k],
            recv_sem=recv_sem.at[k],
            device_id=in_cube(peer(k)),
            device_id_type=pl.DeviceIdType.MESH,
        )

    order = list(range(1, n)) + [0]
    group = 4
    for first in range(0, n, group):
        chosen = order[first:first + group]
        picks = jnp.concatenate(
            [
                jnp.where(
                    lax.broadcasted_iota(jnp.int32, (block, rows), 0) + peer(k) * block == slot,
                    1.0,
                    0.0,
                )
                for k in chosen
            ],
            axis=0,
        )
        packed = jnp.dot(
            picks.astype(jnp.bfloat16), stage[held], preferred_element_type=jnp.float32
        ).astype(jnp.bfloat16)
        filled = jnp.max(picks, axis=1, keepdims=True)
        head = packed[:, :LANES].astype(jnp.float32)
        marked = (lax.broadcasted_iota(jnp.int32, head.shape, 1) == 0) & (filled < 0.5)
        head = jnp.where(marked, EMPTY, head).astype(jnp.bfloat16)
        for i, k in enumerate(chosen):
            piece = slice(i * block, (i + 1) * block)
            if k == 0:
                recv[place, :, :LANES] = head[piece]
                recv[place, :, LANES:] = packed[piece, LANES:]
            else:
                send[k, :, :LANES] = head[piece]
                send[k, :, LANES:] = packed[piece, LANES:]
                block_copy(k).start()

    @pl.when(keeps)
    def _():
        move_ids(1).wait_recv()
        move_ids(1).start()
        for q in range(CHUNKS):
            move(q, 1).wait_recv()
            move(q, 1).start()

    lines = clusters * slots // LANES
    line = own_cid * (slots // LANES) + lax.div(wide * cap, LANES)
    lane = own_rank + lax.rem(wide * cap, LANES)
    own_line = lax.broadcasted_iota(jnp.int32, (lines, rows), 0) == line
    picked[...] = jnp.where(own_line, 1.0, 0.0).astype(jnp.bfloat16)

    def arrived(i, carry):
        kind = lax.div(i, half // 2)
        core_of = lax.rem(lax.div(kind + 1, 2), 2)
        x = lax.rem(guest + lax.rem(kind, 2), 2)
        index = x * half + lax.rem(i, half // 2) * 2 + core_of
        k = lax.rem(me - index + n, n)
        came = block_of(index)

        @pl.when(k != 0)
        def _():
            pltpu.make_async_remote_copy(
                src_ref=send.at[0],
                dst_ref=recv.at[came],
                send_sem=send_sem.at[k],
                recv_sem=recv_sem.at[k],
                device_id=in_cube(index),
                device_id_type=pl.DeviceIdType.MESH,
            ).wait_recv()

        raw = recv[came]
        unit = normalize(raw)
        head = unit[:, :LANES].astype(jnp.float32)
        first = lax.broadcasted_iota(jnp.int32, head.shape, 1) == 0
        marked = first & (raw[:, :LANES].astype(jnp.float32) > EMPTY / 2)
        recv[came, :, :LANES] = jnp.where(marked, EMPTY, head).astype(jnp.bfloat16)
        recv[came, :, LANES:] = unit[:, LANES:]
        return carry

    lax.fori_loop(0, n, arrived, 0)

    step = 256
    for c in range(CLUS_DEV):
        for start in range(0, slots, step):
            top = start + step
            keys = recv[: top // cap, c * cap:(c + 1) * cap, :].reshape(top, width)
            queries = recv[start // cap:top // cap, c * cap:(c + 1) * cap, :].reshape(step, width)
            gram = lax.dot_general(
                keys, queries, (((1,), (1,)), ((), ())), preferred_element_type=jnp.float32
            )
            flag = keys[:, :LANES].astype(jnp.float32)[:, :1]
            position = lax.broadcasted_iota(jnp.int32, (top, 1), 0)
            position = jnp.where(flag < 2.0, position, FAR)
            mine = lax.broadcasted_iota(jnp.int32, (1, step), 1) + start
            best = jnp.max(jnp.where(position < mine, gram, -1.0), axis=0, keepdims=True)
            for at in range(0, step, LANES):
                row = (c * slots + start + at) // LANES
                res[row:row + 1, :] = best[:, at:at + LANES]

    def back_copy(k):
        return pltpu.make_async_remote_copy(
            src_ref=res,
            dst_ref=ret.at[me],
            send_sem=back_send_sem.at[k],
            recv_sem=back_recv_sem.at[me],
            device_id=device(guest, lax.rem(wide + k, n)),
            device_id_type=pl.DeviceIdType.MESH,
        )

    def give_back(k, carry):
        back_copy(k).start()
        return carry

    lax.fori_loop(home, n, give_back, 0)

    @pl.when(home == 1)
    def _():
        ret[me] = res[...]

    move_ids(0).wait_send()
    for q in range(CHUNKS):
        move(q, 0).wait_send()

    def sent(k, carry):
        block_copy(k).wait_send()
        return carry

    lax.fori_loop(1, n, sent, 0)

    def given(k, carry):
        back_copy(k).wait_send()
        return carry

    lax.fori_loop(home, n, given, 0)

    def returned(index, carry):
        @pl.when((home == 0) | (index != me))
        def _():
            pltpu.make_async_remote_copy(
                src_ref=res,
                dst_ref=ret.at[index],
                send_sem=back_send_sem.at[0],
                recv_sem=back_recv_sem.at[index],
                device_id=device(guest, lax.rem(wide + 1, n)),
                device_id_type=pl.DeviceIdType.MESH,
            ).wait_recv()

        return carry

    lax.fori_loop(0, n, returned, 0)

    value = ret[...].reshape(lines, LANES)
    looked = jnp.zeros((LANES, rows), jnp.float32)
    for _ in range(3):
        piece = value.astype(jnp.bfloat16)
        looked = looked + lax.dot_general(
            piece, picked[...], (((0,), (0,)), ((), ())), preferred_element_type=jnp.float32
        )
        value = value - piece.astype(jnp.float32)
    at_lane = lax.broadcasted_iota(jnp.int32, (LANES, rows), 0) == lane
    out_ref[...] = jnp.sum(jnp.where(at_lane, looked, 0.0), axis=0, keepdims=True)


def by_kernel(embeddings, cluster_id):
    rows, width = embeddings.shape
    n = lax.axis_size("wide")
    cap = 2 * rows // (CLUS_DEV * n)
    lines = CLUS_DEV * n * cap // LANES
    out = pl.pallas_call(
        functools.partial(dispatch_kernel, n, cap),
        out_shape=jax.ShapeDtypeStruct((1, rows), jnp.float32),
        in_specs=[pl.BlockSpec(memory_space=pl.ANY)] * 2,
        out_specs=pl.BlockSpec(memory_space=pltpu.VMEM),
        scratch_shapes=[
            pltpu.VMEM((2, rows, width), jnp.bfloat16),
            pltpu.VMEM((2, 1, rows), jnp.int32),
            pltpu.VMEM((n, CLUS_DEV * cap, width), jnp.bfloat16),
            pltpu.VMEM((n, CLUS_DEV * cap, width), jnp.bfloat16),
            pltpu.VMEM((lines, LANES), jnp.float32),
            pltpu.VMEM((n, lines, LANES), jnp.float32),
            pltpu.VMEM((n * lines, rows), jnp.bfloat16),
            pltpu.SemaphoreType.DMA((2,)),
            pltpu.SemaphoreType.DMA((CHUNKS,)),
            pltpu.SemaphoreType.DMA((CHUNKS,)),
            pltpu.SemaphoreType.DMA((2,)),
            pltpu.SemaphoreType.DMA((n,)),
            pltpu.SemaphoreType.DMA((n,)),
            pltpu.SemaphoreType.DMA((n,)),
            pltpu.SemaphoreType.DMA((n,)),
        ],
        compiler_params=pltpu.CompilerParams(
            collective_id=0, has_side_effects=True, vmem_limit_bytes=56 << 20
        ),
    )(embeddings, cluster_id.reshape(1, rows))
    return out.reshape(rows)


def by_collectives(embeddings, cluster_id):
    row_count = embeddings.shape[0]
    wide_count = lax.axis_size("wide")
    per_owner = CLUS_DEV
    capacity = 2 * row_count // (per_owner * wide_count)
    cluster_count = per_owner * wide_count
    total_slots = cluster_count * capacity
    cluster_ids = cluster_id[:, 0]
    onehot = (cluster_ids[:, None] == jnp.arange(cluster_count, dtype=jnp.int32)[None, :]).astype(
        jnp.int32
    )
    earlier = jnp.cumsum(onehot, axis=0) - onehot
    place_rank = jnp.sum(earlier * onehot, axis=1)
    slot_index = cluster_ids * capacity + place_rank
    source_row = (
        jnp.zeros((total_slots,), jnp.int32)
        .at[slot_index]
        .set(jnp.arange(row_count, dtype=jnp.int32))
    )
    filled_flags = jnp.zeros((total_slots,), jnp.bfloat16).at[slot_index].set(jnp.bfloat16(1.0))
    packed = embeddings[source_row].reshape(wide_count, per_owner, capacity, embeddings.shape[1])
    flag_blocks = filled_flags.reshape(wide_count, per_owner, capacity)
    received = lax.all_to_all(packed, "wide", split_axis=0, concat_axis=2, tiled=True)
    flags_here = lax.all_to_all(flag_blocks, "wide", split_axis=0, concat_axis=2, tiled=True)
    unit = normalize(received)
    slot_total = unit.shape[2]
    live = flags_here > 0
    gram = jnp.einsum("pksd,pktd->pkst", unit, unit, preferred_element_type=jnp.float32)
    positions = jnp.arange(slot_total, dtype=jnp.int32)
    mask = (positions[None, :] < positions[:, None])[None, None] & live[:, :, None, :]
    maxima = jnp.max(jnp.where(mask, gram, jnp.float32(-1.0)), axis=3)
    returned = lax.all_to_all(maxima, "wide", split_axis=2, concat_axis=0, tiled=True)
    return returned.reshape(total_slots)[slot_index]


def per_device(embeddings, cluster_id):
    rows, width = embeddings.shape
    n = lax.axis_size("wide")
    cap = 2 * rows // (CLUS_DEV * n)
    if lax.axis_size("parts") == 2 and n == 16 and cap == 32 and width % LANES == 0:
        return by_kernel(embeddings, cluster_id)
    return by_collectives(embeddings, cluster_id)


def solution(mesh):
    in_specs = (P(("parts", "wide"), None), P(("parts", "wide"), None))
    out_specs = P(("parts", "wide"))
    return jax.shard_map(
        per_device, mesh=mesh, in_specs=in_specs, out_specs=out_specs, check_vma=False
    )
```

time: 61.9 us -> 73.4 us (1.19)
  Pallas kernels: 59.3 us -> 71.9 us
  local copies, waits for them, and re-layouts: 2.49 us -> 1.26 us
    pallas_call x1, Pallas kernels: 59.3 us -> 71.9 us  [by_kernel(): pl.pallas_call(functools.partial(dispatch_kernel, n, cap), out_shape=jax....]
    unnamed x5 -> x1, local copies, waits for them, and re-layouts: 2.49 us -> 1.26 us
where the time goes in v2:
time: 73.4 us; the launch traced here: 73.2 us
  Pallas kernels  71.9 us (98%)
  local copies, waits for them, and re-layouts  1.26 us (2%)
    pallas_call x1, Pallas kernels, by_kernel(): pl.pallas_call(functools.partial(dispatch_kernel, n, cap), out_shape=jax....  71.9 us

profile of v2, /device:TPU:0, one launch (start us, length us, event | category | flops | bytes accessed | tf_op | source)
XLA Modules:
  0.0 73.2 jit_solution(773988701536330171)
XLA Ops:
  0.0 71.9 %shard_map.28 = f32[1,512]{1,0:T(1,128)} custom-call(bf16[512,1024]{1,0:T(8,128)(2,1)} %emb_ref.1, s32[1,512]{1,0:T(1,128)} %bitcast.3), custom_call_target="tpu_custom_call" | custom-call | tf_op jit(solution)/shard_map/pallas_call | solution.py:310
  71.9 1.3 %copy.4 = f32[512]{0:T(512)} copy(f32[512]{0:T(512)} %bitcast.2) | data formatting | bytes 4096

commit v3 on v1

--- a/solution.py
+++ b/solution.py
@@ -11,6 +11,8 @@
 LANES = 128
 EMPTY = 4.0
 FAR = 1 << 20
+GROUPS = (4, 4, 4, 4)
+EARLY = 4
 
 
 def normalize(values):
@@ -20,17 +22,34 @@
 
 
 def dispatch_kernel(
-    n, cap, emb_ref, cid_ref, out_ref, unit, send, recv, res, ret,
-    send_sem, recv_sem, back_send_sem, back_recv_sem,
+    n, cap, emb_ref, cid_ref, out_ref, rows_here, ids, before, send, recv, res, ret, picked,
+    local_sem, send_sem, recv_sem, back_send_sem, back_recv_sem,
 ):
     me = lax.axis_index("wide")
+    half = n // 2
+    side = lax.div(me, half)
+    spot = lax.rem(me, half)
     rows, width = emb_ref.shape
     block = CLUS_DEV * cap
     slots = n * cap
     clusters = CLUS_DEV * n
 
     def peer(k):
-        return lax.rem(me + k, n)
+        base = jnp.where(k < half, 1 - side, side) * half
+        return base + lax.rem(spot + lax.rem(k, half), half)
+
+    def source(k):
+        base = jnp.where(k < half, 1 - side, side) * half
+        return base + lax.rem(spot + half - lax.rem(k, half), half)
+
+    def partners(body):
+        lax.fori_loop(0, half, body, 0)
+        lax.fori_loop(half + 1, n, body, 0)
+
+    get_ids = pltpu.make_async_copy(cid_ref, ids, local_sem.at[0])
+    get_rows = pltpu.make_async_copy(emb_ref, rows_here, local_sem.at[1])
+    get_ids.start()
+    get_rows.start()
 
     barrier = pltpu.get_barrier_semaphore()
 
@@ -40,28 +59,24 @@
         )
         return carry
 
-    lax.fori_loop(1, n, greet, 0)
-
-    def unit_rows(t, carry):
-        part = pl.ds(pl.multiple_of(t * 64, 64), 64)
-        unit[part, :] = normalize(emb_ref[part, :])
-        return carry
-
-    lax.fori_loop(0, rows // 64, unit_rows, 0)
-    cid = cid_ref[...]
+    partners(greet)
+
+    earlier_row = lax.broadcasted_iota(jnp.int32, (rows, rows), 0) < lax.broadcasted_iota(
+        jnp.int32, (rows, rows), 1
+    )
+    before[...] = jnp.where(earlier_row, 1.0, 0.0).astype(jnp.bfloat16)
+    get_ids.wait()
+    cid = ids[...]
     named = lax.broadcasted_iota(jnp.int32, (clusters, rows), 0) == cid
-    before = lax.broadcasted_iota(jnp.int32, (rows, rows), 0) < lax.broadcasted_iota(
-        jnp.int32, (rows, rows), 1
-    )
     earlier = jnp.dot(
         jnp.where(named, 1.0, 0.0).astype(jnp.bfloat16),
-        jnp.where(before, 1.0, 0.0).astype(jnp.bfloat16),
+        before[...],
         preferred_element_type=jnp.float32,
     )
     rank = jnp.sum(jnp.where(named, earlier, 0.0), axis=0, keepdims=True).astype(jnp.int32)
     slot = cid * cap + rank
 
-    pl.semaphore_wait(barrier, n - 1)
+    get_rows.wait()
 
     def block_copy(k, place):
         return pltpu.make_async_remote_copy(
@@ -73,9 +88,12 @@
             device_id_type=pl.DeviceIdType.MESH,
         )
 
-    order = sorted(range(n), key=lambda k: (abs(k - n // 2), k))
-    group = 4
-    for first in range(0, n, group):
+    order = [0]
+    for k in range(1, half):
+        order += [half + k, k]
+    order.append(half)
+    first = 0
+    for group in GROUPS:
         chosen = order[first:first + group]
         picks = jnp.concatenate(
             [
@@ -89,26 +107,42 @@
             axis=0,
         )
         packed = jnp.dot(
-            picks.astype(jnp.bfloat16), unit[...], preferred_element_type=jnp.float32
-        ).astype(jnp.bfloat16)
+            picks.astype(jnp.bfloat16), rows_here[...], preferred_element_type=jnp.float32
+        )
+        packed = normalize(packed)
         filled = jnp.max(picks, axis=1, keepdims=True)
         head = packed[:, :LANES].astype(jnp.float32)
         marked = (lax.broadcasted_iota(jnp.int32, head.shape, 1) == 0) & (filled < 0.5)
         head = jnp.where(marked, EMPTY, head).astype(jnp.bfloat16)
         for i, k in enumerate(chosen):
             part = slice(i * block, (i + 1) * block)
-            if k == 0:
+            if k == half:
                 recv[me, :, :LANES] = head[part]
                 recv[me, :, LANES:] = packed[part, LANES:]
             else:
                 send[first + i, :, :LANES] = head[part]
                 send[first + i, :, LANES:] = packed[part, LANES:]
-                block_copy(k, first + i).start()
+        first += group
+        if first == EARLY:
+            pl.semaphore_wait(barrier, n - 1)
+            for i, k in enumerate(order[:first]):
+                block_copy(k, i).start()
+        elif first > EARLY:
+            for i, k in enumerate(chosen):
+                if k != half:
+                    block_copy(k, first - group + i).start()
+
+    lines = clusters * slots // LANES
+    place = me * cap
+    line = cid * (slots // LANES) + lax.div(place, LANES)
+    lane = rank + lax.rem(place, LANES)
+    own_line = lax.broadcasted_iota(jnp.int32, (lines, rows), 0) == line
+    picked[...] = jnp.where(own_line, 1.0, 0.0).astype(jnp.bfloat16)
 
     def arrived(k, carry):
         pltpu.make_async_remote_copy(
             src_ref=send.at[0],
-            dst_ref=recv.at[lax.rem(me + n - k, n)],
+            dst_ref=recv.at[source(k)],
             send_sem=send_sem.at[k],
             recv_sem=recv_sem.at[k],
             device_id={"wide": peer(k)},
@@ -116,25 +150,41 @@
         ).wait_recv()
         return carry
 
-    lax.fori_loop(1, n, arrived, 0)
-
-    step = 256
+    step = slots // 2
+
+    def largest(c, k, q, within):
+        def slots_of(h):
+            blocks = recv[pl.ds(h * half, half), c * cap:(c + 1) * cap, :]
+            return blocks.reshape(step, width)
+
+        keys = slots_of(k)
+        gram = lax.dot_general(
+            keys, slots_of(q), (((1,), (1,)), ((), ())), preferred_element_type=jnp.float32
+        )
+        flag = keys[:, :LANES].astype(jnp.float32)[:, :1]
+        position = lax.broadcasted_iota(jnp.int32, (step, 1), 0) if within else 0
+        position = jnp.where(flag < 2.0, position, FAR)
+        mine = lax.broadcasted_iota(jnp.int32, (1, step), 1) if within else 1
+        return jnp.max(jnp.where(position < mine, gram, -1.0), axis=0, keepdims=True)
+
+    def within_half(h):
+        for c in range(CLUS_DEV):
+            best = largest(c, h, h, True)
+            for i in range(step // LANES):
+                row = (c * slots + h * step) // LANES + i
+                res[pl.ds(row, 1), :] = best[:, i * LANES:(i + 1) * LANES]
+
+    lax.fori_loop(half + 1, n, arrived, 0)
+    within_half(side)
+    lax.fori_loop(0, half, arrived, 0)
+    within_half(1 - side)
     for c in range(CLUS_DEV):
-        for start in range(0, slots, step):
-            top = start + step
-            keys = recv[: top // cap, c * cap:(c + 1) * cap, :].reshape(top, width)
-            queries = recv[start // cap:top // cap, c * cap:(c + 1) * cap, :].reshape(step, width)
-            gram = lax.dot_general(
-                keys, queries, (((1,), (1,)), ((), ())), preferred_element_type=jnp.float32
+        best = largest(c, 0, 1, False)
+        for i in range(step // LANES):
+            row = (c * slots + step) // LANES + i
+            res[row:row + 1, :] = jnp.maximum(
+                res[row:row + 1, :], best[:, i * LANES:(i + 1) * LANES]
             )
-            flag = keys[:, :LANES].astype(jnp.float32)[:, :1]
-            position = lax.broadcasted_iota(jnp.int32, (top, 1), 0)
-            position = jnp.where(flag < 2.0, position, FAR)
-            mine = lax.broadcasted_iota(jnp.int32, (1, step), 1) + start
-            best = jnp.max(jnp.where(position < mine, gram, -1.0), axis=0, keepdims=True)
-            for lane in range(0, step, LANES):
-                row = (c * slots + start + lane) // LANES
-                res[row:row + 1, :] = best[:, lane:lane + LANES]
 
     def back_copy(k):
         return pltpu.make_async_remote_copy(
@@ -150,19 +200,19 @@
         back_copy(k).start()
         return carry
 
-    lax.fori_loop(1, n, give_back, 0)
+    partners(give_back)
     ret[me] = res[...]
 
     def sent(k, carry):
         block_copy(k, 0).wait_send()
         return carry
 
-    lax.fori_loop(1, n, sent, 0)
+    partners(sent)
 
     def returned(k, carry):
         pltpu.make_async_remote_copy(
             src_ref=res,
-            dst_ref=ret.at[lax.rem(me + n - k, n)],
+            dst_ref=ret.at[source(k)],
             send_sem=back_send_sem.at[k],
             recv_sem=back_recv_sem.at[k],
             device_id={"wide": peer(k)},
@@ -170,20 +220,14 @@
         ).wait()
         return carry
 
-    lax.fori_loop(1, n, returned, 0)
-
-    lines = clusters * slots // LANES
+    partners(returned)
+
     value = ret[...].reshape(lines, LANES)
-    place = me * cap
-    line = cid * (slots // LANES) + lax.div(place, LANES)
-    lane = rank + lax.rem(place, LANES)
-    chosen = (lax.broadcasted_iota(jnp.int32, (lines, rows), 0) == line)
-    chosen = jnp.where(chosen, 1.0, 0.0).astype(jnp.bfloat16)
     looked = jnp.zeros((LANES, rows), jnp.float32)
     for _ in range(3):
         piece = value.astype(jnp.bfloat16)
         looked = looked + lax.dot_general(
-            piece, chosen, (((0,), (0,)), ((), ())), preferred_element_type=jnp.float32
+            piece, picked[...], (((0,), (0,)), ((), ())), preferred_element_type=jnp.float32
         )
         value = value - piece.astype(jnp.float32)
     at_lane = lax.broadcasted_iota(jnp.int32, (LANES, rows), 0) == lane
@@ -198,21 +242,25 @@
     out = pl.pallas_call(
         functools.partial(dispatch_kernel, n, cap),
         out_shape=jax.ShapeDtypeStruct((1, rows), jnp.float32),
-        in_specs=[pl.BlockSpec(memory_space=pltpu.VMEM)] * 2,
+        in_specs=[pl.BlockSpec(memory_space=pl.ANY)] * 2,
         out_specs=pl.BlockSpec(memory_space=pltpu.VMEM),
         scratch_shapes=[
             pltpu.VMEM((rows, width), jnp.bfloat16),
+            pltpu.VMEM((1, rows), jnp.int32),
+            pltpu.VMEM((rows, rows), jnp.bfloat16),
             pltpu.VMEM((n, CLUS_DEV * cap, width), jnp.bfloat16),
             pltpu.VMEM((n, CLUS_DEV * cap, width), jnp.bfloat16),
             pltpu.VMEM((lines, LANES), jnp.float32),
             pltpu.VMEM((n, lines, LANES), jnp.float32),
+            pltpu.VMEM((n * lines, rows), jnp.bfloat16),
+            pltpu.SemaphoreType.DMA((2,)),
             pltpu.SemaphoreType.DMA((n,)),
             pltpu.SemaphoreType.DMA((n,)),
             pltpu.SemaphoreType.DMA((n,)),
             pltpu.SemaphoreType.DMA((n,)),
         ],
         compiler_params=pltpu.CompilerParams(
-            collective_id=0, has_side_effects=True, vmem_limit_bytes=40 << 20
+            collective_id=0, has_side_effects=True, vmem_limit_bytes=56 << 20
         ),
     )(embeddings, cluster_id.reshape(1, rows))
     return out.reshape(rows)
@@ -257,7 +305,7 @@
     rows, width = embeddings.shape
     n = lax.axis_size("wide")
     cap = 2 * rows // (CLUS_DEV * n)
-    if cap % 16 == 0 and n % 4 == 0 and (n * cap) % 256 == 0 and 256 % cap == 0 and width % LANES == 0:
+    if n == 16 and cap == 32 and width % LANES == 0:
         return by_kernel(embeddings, cluster_id)
     return by_collectives(embeddings, cluster_id)
 

time: 61.9 us -> 60.2 us (0.973)
  local copies, waits for them, and re-layouts: 2.49 us -> 1.26 us
    unnamed x5 -> x1, local copies, waits for them, and re-layouts: 2.49 us -> 1.26 us
where the time goes in v3:
time: 60.2 us; the launch traced here: 60.1 us
  Pallas kernels  58.8 us (98%)
  local copies, waits for them, and re-layouts  1.26 us (2%)
    pallas_call x1, Pallas kernels, by_kernel(): pl.pallas_call(functools.partial(dispatch_kernel, n, cap), out_shape=jax....  58.8 us
    unnamed x1, local copies, waits for them, and re-layouts  1.26 us

profile of v3, /device:TPU:0, one launch (start us, length us, event | category | flops | bytes accessed | tf_op | source)
XLA Modules:
  0.0 60.1 jit_solution(6358206048985279315)
XLA Ops:
  0.0 58.8 %shard_map.28 = f32[1,512]{1,0:T(1,128)} custom-call(bf16[512,1024]{1,0:T(8,128)(2,1)} %emb_ref.1, s32[1,512]{1,0:T(1,128)} %bitcast.3), custom_call_target="tpu_custom_call" | custom-call | tf_op jit(solution)/shard_map/pallas_call | solution.py:242
  58.8 1.3 %copy.4 = f32[512]{0:T(512)} copy(f32[512]{0:T(512)} %bitcast.2) | data formatting | bytes 4096

commit v4 on v3

--- a/solution.py
+++ b/solution.py
@@ -130,6 +130,8 @@
         elif first > EARLY:
             for i, k in enumerate(chosen):
                 if k != half:
+                    if k < half and k >= 5:
+                        block_copy(k - 5, 0).wait_send()
                     block_copy(k, first - group + i).start()
 
     lines = clusters * slots // LANES
@@ -207,7 +209,8 @@
         block_copy(k, 0).wait_send()
         return carry
 
-    partners(sent)
+    lax.fori_loop(3, half, sent, 0)
+    lax.fori_loop(half + 1, n, sent, 0)
 
     def returned(k, carry):
         pltpu.make_async_remote_copy(

time: 60.2 us -> 60.2 us (level)
  no operation moved by 1% of the time
where the time goes in v4:
time: 60.2 us; the launch traced here: 60.1 us
  Pallas kernels  58.8 us (98%)
  local copies, waits for them, and re-layouts  1.26 us (2%)
    pallas_call x1, Pallas kernels, by_kernel(): pl.pallas_call(functools.partial(dispatch_kernel, n, cap), out_shape=jax....  58.8 us
    unnamed x1, local copies, waits for them, and re-layouts  1.26 us

profile of v4, /device:TPU:0, one launch (start us, length us, event | category | flops | bytes accessed | tf_op | source)
XLA Modules:
  0.0 60.1 jit_solution(7776206408226404156)
XLA Ops:
  0.0 58.8 %shard_map.28 = f32[1,512]{1,0:T(1,128)} custom-call(bf16[512,1024]{1,0:T(8,128)(2,1)} %emb_ref.1, s32[1,512]{1,0:T(1,128)} %bitcast.3), custom_call_target="tpu_custom_call" | custom-call | tf_op jit(solution)/shard_map/pallas_call | solution.py:245
  58.8 1.3 %copy.4 = f32[512]{0:T(512)} copy(f32[512]{0:T(512)} %bitcast.2) | data formatting | bytes 4096
